TPU v7x, 128 devices: a whole 4x4x4 slice. The times are simulated.
128 devices in a mesh: dp: 4 (over y), seq: 32 (over x, z, core).
Axes of the slice: x: 4, y: 4, z: 4, core: 2. Of those that a mesh axis runs over, the one named last changes fastest.
Arguments:
- queries: bfloat16 [16384, 4096], P(('dp', 'seq')), parts along dimension 0, may hold values from -6 to 6
- key_codes: bfloat16 [16384, 1024], P(('dp', 'seq')), parts along dimension 0, may hold values from -6 to 6
- key_block_scale: bfloat16 [128, 8], P(('dp', 'seq')), parts along dimension 0, may hold values from 0.5 to 2
- value_code_matrix: bfloat16 [16384, 1024], P(('dp', 'seq')), parts along dimension 0, may hold values from -6 to 6
- value_block_scale: bfloat16 [128, 8], P(('dp', 'seq')), parts along dimension 0, may hold values from 0.5 to 2
- attn_out: bfloat16 [16384, 4096], P(('dp', 'seq')), parts along dimension 0, may hold values from -4 to 4
- out_grad: bfloat16 [16384, 4096], P(('dp', 'seq')), parts along dimension 0, may hold values from -6 to 6
Outputs:
- query_grad: bfloat16 [16384, 4096], P(('dp', 'seq')), parts along dimension 0
- dequant_key_gradient: bfloat16 [16384, 1024], P(('dp', 'seq')), parts along dimension 0
- dequant_value_gradient: bfloat16 [16384, 1024], P(('dp', 'seq')), parts along dimension 0
There are 4 independent parts, one for each index of `dp`. A program takes and returns all parts, laid end to end along the dimension named above; each array names one. Nothing has to cross between parts.
All inputs are finite; a program needn't handle non-finite values.
Results may differ from a plain program's by a relative error of at most 0.0014.
The roundings to bfloat16 on the way count: a program that leaves them out, or rounds other values in their place, can miss the bound.
Values may be sent and summed in bfloat16 or wider, within the bound.
A program may use at most 128 MiB of HBM per device.

v0:
```python
import jax
import jax.numpy as jnp
from jax import lax
from jax.sharding import PartitionSpec as P

QUERY_HEADS = 32
KEY_VALUE_HEADS = 8
HEAD_WIDTH = 128
SCALE_BLOCK_SPAN = 128


def spread_kv(input_tensor, inner_product):
    row_count_total = input_tensor.shape[0]
    head_copies = lax.axis_size("seq") // KEY_VALUE_HEADS
    split_pieces = input_tensor.reshape(row_count_total, KEY_VALUE_HEADS, inner_product)
    spread_heads = jnp.broadcast_to(
        split_pieces[:, :, None, :], (row_count_total, KEY_VALUE_HEADS, head_copies, inner_product)
    )
    return spread_heads.reshape(row_count_total, KEY_VALUE_HEADS * head_copies * inner_product)


def fold_kv(input_tensor):
    row_count_total = input_tensor.shape[0]
    head_copies = lax.axis_size("seq") // KEY_VALUE_HEADS
    folded_heads = jnp.sum(
        input_tensor.reshape(row_count_total, KEY_VALUE_HEADS, head_copies, HEAD_WIDTH), axis=2
    )
    return folded_heads.reshape(row_count_total, KEY_VALUE_HEADS * HEAD_WIDTH)


def dequantize(code_entries, scales):
    seq_len = code_entries.shape[0]
    block_groups = code_entries.astype(jnp.float32).reshape(
        seq_len // SCALE_BLOCK_SPAN, SCALE_BLOCK_SPAN, HEAD_WIDTH
    )
    block_groups = block_groups * scales.astype(jnp.float32)[:, :, None]
    return block_groups.reshape(seq_len, HEAD_WIDTH).astype(jnp.bfloat16)


def per_device(
    queries, key_codes, key_block_scale, value_code_matrix, value_block_scale, attn_out, out_grad
):
    per_dev = QUERY_HEADS // lax.axis_size("seq")
    moved = (
        lax.all_to_all(
            spread_kv(key_codes, HEAD_WIDTH), "seq", split_axis=1, concat_axis=0, tiled=True
        ),
        lax.all_to_all(
            spread_kv(value_code_matrix, HEAD_WIDTH), "seq", split_axis=1, concat_axis=0, tiled=True
        ),
        lax.all_to_all(
            spread_kv(key_block_scale, 1), "seq", split_axis=1, concat_axis=0, tiled=True
        ),
        lax.all_to_all(
            spread_kv(value_block_scale, 1), "seq", split_axis=1, concat_axis=0, tiled=True
        ),
    )
    key_full = dequantize(moved[0], moved[2])
    value_full = dequantize(moved[1], moved[3])
    query_all, grad_all, out_all = (
        lax.all_to_all(queries, "seq", split_axis=1, concat_axis=0, tiled=True),
        lax.all_to_all(out_grad, "seq", split_axis=1, concat_axis=0, tiled=True),
        lax.all_to_all(attn_out, "seq", split_axis=1, concat_axis=0, tiled=True),
    )
    seq_len = query_all.shape[0]
    products = grad_all.astype(jnp.float32) * out_all.astype(jnp.float32)
    row_delta = jnp.sum(products.reshape(seq_len, per_dev, HEAD_WIDTH), axis=2)
    query_heads = query_all.reshape(seq_len, per_dev, HEAD_WIDTH)
    grad_heads = grad_all.reshape(seq_len, per_dev, HEAD_WIDTH)
    softmax_scale = HEAD_WIDTH ** (-0.5)
    block_rows = min(seq_len, max(512, seq_len // 8))
    key_acc = jnp.zeros((seq_len, HEAD_WIDTH), jnp.float32)
    value_acc = jnp.zeros((seq_len, HEAD_WIDTH), jnp.float32)
    query_parts = []
    for block_num in range(seq_len // block_rows):
        first_row = block_num * block_rows
        last_row = first_row + block_rows
        query_blk = query_heads[first_row:last_row]
        grad_blk = grad_heads[first_row:last_row]
        delta_blk = jnp.transpose(row_delta[first_row:last_row])[:, :, None]
        key_blk = key_full[:last_row]
        value_blk = value_full[:last_row]
        scores = (
            jnp.einsum("qhd,kd->hqk", query_blk, key_blk, preferred_element_type=jnp.float32)
            * softmax_scale
        )
        row_pos = first_row + jnp.arange(block_rows)
        causal = row_pos[:, None] >= jnp.arange(last_row)[None, :]
        scores = jnp.where(causal[None], scores, -jnp.inf)
        row_max = jnp.max(scores, axis=2, keepdims=True)
        expo = jnp.exp(scores - row_max)
        row_total = jnp.sum(expo, axis=2, keepdims=True)
        attn_prob = expo / row_total
        prob_bf = attn_prob.astype(jnp.bfloat16)
        value_acc = value_acc.at[:last_row].add(
            jnp.einsum("hqk,qhd->kd", prob_bf, grad_blk, preferred_element_type=jnp.float32)
        )
        prob_grad = jnp.einsum(
            "qhd,kd->hqk", grad_blk, value_blk, preferred_element_type=jnp.float32
        )
        score_grad = (attn_prob * (prob_grad - delta_blk) * softmax_scale).astype(jnp.bfloat16)
        query_parts.append(
            jnp.einsum(
                "hqk,kd->qhd", score_grad, key_blk, preferred_element_type=jnp.float32
            ).astype(jnp.bfloat16)
        )
        key_acc = key_acc.at[:last_row].add(
            jnp.einsum("hqk,qhd->kd", score_grad, query_blk, preferred_element_type=jnp.float32)
        )
    query_local = jnp.concatenate(query_parts, axis=0).reshape(seq_len, per_dev * HEAD_WIDTH)
    query_back = lax.all_to_all(query_local, "seq", split_axis=0, concat_axis=1, tiled=True)
    key_back, value_back = (
        lax.all_to_all(key_acc, "seq", split_axis=0, concat_axis=1, tiled=True),
        lax.all_to_all(value_acc, "seq", split_axis=0, concat_axis=1, tiled=True),
    )
    dequant_key_gradient = fold_kv(key_back).astype(jnp.bfloat16)
    dequant_value_gradient = fold_kv(value_back).astype(jnp.bfloat16)
    return (query_back, dequant_key_gradient, dequant_value_gradient)


def solution(mesh):
    in_specs = (
        P(("dp", "seq"), None),
        P(("dp", "seq"), None),
        P(("dp", "seq"), None),
        P(("dp", "seq"), None),
        P(("dp", "seq"), None),
        P(("dp", "seq"), None),
        P(("dp", "seq"), None),
    )
    out_specs = (P(("dp", "seq"), None), P(("dp", "seq"), None), P(("dp", "seq"), None))
    return jax.shard_map(
        per_device, mesh=mesh, in_specs=in_specs, out_specs=out_specs, check_vma=False
    )
```

profile of v0, /device:TPU:1, one launch (start us, length us, event | category | flops | bytes accessed | tf_op | source)
XLA Modules:
  0.0 287.3 jit_solution(5476687629824600398)
XLA Ops:
  2.1 9.4 %all-to-all-start.4 = ((bf16[1,32,1]{2,0,1:T(2,128)(2,1)}), bf16[1,32,1]{2,0,1:T(2,128)(2,1)S(1)}, u32[]{:S(2)}, u32[]{:S(2)}) async-start(bf16[1,32,1]{2,0,1:T(2,128)(2,1)} %broadcast_in_dim.125), calls=%async_computation.4 | async-start | bytes 32768 | tf_op jit(solution)/shard_map/all_to_all | solution.py:54
  13.0 5.5 %all-to-all-done.4 = bf16[1,32,1]{2,0,1:T(2,128)(2,1)S(1)} async-done(((bf16[1,32,1]{2,0,1:T(2,128)(2,1)}), bf16[1,32,1]{2,0,1:T(2,128)(2,1)S(1)}, u32[]{:S(2)}, u32[]{:S(2)}) %all-to-all-start.4) | async-done | bytes 96 | tf_op jit(solution)/shard_map/all_to_all | solution.py:54
  18.4 4.1 %all-to-all-start.1 = ((bf16[1,32,1]{2,0,1:T(2,128)(2,1)}), bf16[1,32,1]{2,0,1:T(2,128)(2,1)S(1)}, u32[]{:S(2)}, u32[]{:S(2)}) async-start(bf16[1,32,1]{2,0,1:T(2,128)(2,1)} %broadcast_in_dim.124), calls=%async_computation.1 | async-start | bytes 32768 | tf_op jit(solution)/shard_map/all_to_all | solution.py:51
  22.6 6.9 %all-to-all-done.1 = bf16[1,32,1]{2,0,1:T(2,128)(2,1)S(1)} async-done(((bf16[1,32,1]{2,0,1:T(2,128)(2,1)}), bf16[1,32,1]{2,0,1:T(2,128)(2,1)S(1)}, u32[]{:S(2)}, u32[]{:S(2)}) %all-to-all-start.1) | async-done | bytes 96 | tf_op jit(solution)/shard_map/all_to_all | solution.py:51
  30.8 4.4 %all-to-all-start.3 = ((bf16[128,32,128]{2,0,1:T(8,128)(2,1)}), bf16[128,32,128]{2,0,1:T(8,128)(2,1)S(1)}, u32[]{:S(2)}, u32[]{:S(2)}) async-start(bf16[128,32,128]{2,0,1:T(8,128)(2,1)} %bitcast.9), calls=%async_computation.3 | async-start | bytes 2097152 | tf_op jit(solution)/shard_map/all_to_all | solution.py:48
  35.2 16.9 %all-to-all-done.3 = bf16[128,32,128]{2,0,1:T(8,128)(2,1)S(1)} async-done(((bf16[128,32,128]{2,0,1:T(8,128)(2,1)}), bf16[128,32,128]{2,0,1:T(8,128)(2,1)S(1)}, u32[]{:S(2)}, u32[]{:S(2)}) %all-to-all-start.3) | async-done | bytes 1048608 | tf_op jit(solution)/shard_map/all_to_all | solution.py:48
  53.5 3.9 %all-to-all-start = ((bf16[128,32,128]{2,0,1:T(8,128)(2,1)}), bf16[128,32,128]{2,0,1:T(8,128)(2,1)S(1)}, u32[]{:S(2)}, u32[]{:S(2)}) async-start(bf16[128,32,128]{2,0,1:T(8,128)(2,1)} %bitcast), calls=%async_computation | async-start | bytes 2097152 | tf_op jit(solution)/shard_map/all_to_all | solution.py:45
  58.8 15.6 %all-to-all-done = bf16[128,32,128]{2,0,1:T(8,128)(2,1)S(1)} async-done(((bf16[128,32,128]{2,0,1:T(8,128)(2,1)}), bf16[128,32,128]{2,0,1:T(8,128)(2,1)S(1)}, u32[]{:S(2)}, u32[]{:S(2)}) %all-to-all-start) | async-done | bytes 1048608 | tf_op jit(solution)/shard_map/all_to_all | solution.py:45
  74.3 4.0 %all-to-all-start.2 = ((bf16[128,32,128]{0,2,1:T(8,128)(2,1)}), bf16[128,32,128]{0,2,1:T(8,128)(2,1)S(1)}, u32[]{:S(2)}, u32[]{:S(2)}) async-start(bf16[128,32,128]{0,2,1:T(8,128)(2,1)} %bitcast.439), calls=%async_computation.2 | async-start | bytes 2097152 | tf_op jit(solution)/shard_map/all_to_all | solution.py:61
  78.3 2.3 copy.67
  80.6 14.6 %all-to-all-done.2 = bf16[128,32,128]{0,2,1:T(8,128)(2,1)S(1)} async-done(((bf16[128,32,128]{0,2,1:T(8,128)(2,1)}), bf16[128,32,128]{0,2,1:T(8,128)(2,1)S(1)}, u32[]{:S(2)}, u32[]{:S(2)}) %all-to-all-start.2) | async-done | bytes 1048608 | tf_op jit(solution)/shard_map/all_to_all | solution.py:61
  96.2 4.0 %all-to-all-start.5 = ((bf16[128,32,128]{0,2,1:T(8,128)(2,1)}), bf16[128,32,128]{0,2,1:T(8,128)(2,1)S(1)}, u32[]{:S(2)}, u32[]{:S(2)}) async-start(bf16[128,32,128]{0,2,1:T(8,128)(2,1)} %bitcast.438), calls=%async_computation.5 | async-start | bytes 2097152 | tf_op jit(solution)/shard_map/all_to_all | solution.py:62
  100.2 2.3 copy.69
  107.2 9.9 %all-to-all-done.5 = bf16[128,32,128]{0,2,1:T(8,128)(2,1)S(1)} async-done(((bf16[128,32,128]{0,2,1:T(8,128)(2,1)}), bf16[128,32,128]{0,2,1:T(8,128)(2,1)S(1)}, u32[]{:S(2)}, u32[]{:S(2)}) %all-to-all-start.5) | async-done | bytes 1048608 | tf_op jit(solution)/shard_map/all_to_all | solution.py:62
  117.1 4.6 %all-to-all-start.6 = ((bf16[128,32,128]{0,2,1:T(8,128)(2,1)}), bf16[128,32,128]{0,2,1:T(8,128)(2,1)}, u32[]{:S(2)}, u32[]{:S(2)}) async-start(bf16[128,32,128]{0,2,1:T(8,128)(2,1)} %bitcast.436), calls=%async_computation.6 | async-start | bytes 2097152 | tf_op jit(solution)/shard_map/all_to_all | solution.py:63
  130.2 8.4 %all-to-all-done.6 = bf16[128,32,128]{0,2,1:T(8,128)(2,1)} async-done(((bf16[128,32,128]{0,2,1:T(8,128)(2,1)}), bf16[128,32,128]{0,2,1:T(8,128)(2,1)}, u32[]{:S(2)}, u32[]{:S(2)}) %all-to-all-start.6) | async-done | bytes 1048608 | tf_op jit(solution)/shard_map/all_to_all | solution.py:63
  138.5 1.6 fusion.58
  169.5 1.5 fusion.24
  176.0 2.3 fusion.25
  183.9 2.2 fusion.12
  193.1 2.4 fusion.13
  198.9 4.2 %all-to-all-start.7 = ((bf16[32,128,128]{1,2,0:T(8,128)(2,1)}), bf16[32,128,128]{1,2,0:T(8,128)(2,1)S(1)}, u32[]{:S(2)}, u32[]{:S(2)}) async-start(bf16[32,128,128]{1,2,0:T(8,128)(2,1)} %copy.84), calls=%async_computation.7 | async-start | bytes 2097152 | tf_op jit(solution)/shard_map/all_to_all | solution.py:111
  203.1 6.9 %convolution_add_fusion.2 = f32[4096,128]{1,0:T(8,128)} fusion(f32[4096,128]{1,0:T(8,128)} %copy-done.25, bf16[512,128]{1,0:T(8,128)(2,1)S(1)} %bitcast.479, f32[1,512,4096]{1,2,0:T(8,128)} %copy-done.17, f32[512]{0:T(512)S(1)} %fusion.3, f32[512]{0:T(512)S(1)} %get-tuple-element.255), kind=kOutput, calls=%fused_computation.40 | convolution fusion | flops 543686656 | bytes 12718080 | tf_op jit(solution)/shard_map/hqk,qhd->kd/dot_general | solution.py:96
  210.0 9.9 %all-to-all-done.7 = bf16[32,128,128]{1,2,0:T(8,128)(2,1)S(1)} async-done(((bf16[32,128,128]{1,2,0:T(8,128)(2,1)}), bf16[32,128,128]{1,2,0:T(8,128)(2,1)S(1)}, u32[]{:S(2)}, u32[]{:S(2)}) %all-to-all-start.7) | async-done | bytes 1048608 | tf_op jit(solution)/shard_map/all_to_all | solution.py:111
  220.0 4.7 %all-to-all-start.9 = ((f32[32,128,128]{2,1,0:T(8,128)}), f32[32,128,128]{2,1,0:T(8,128)}, u32[]{:S(2)}, u32[]{:S(2)}) async-start(f32[32,128,128]{2,1,0:T(8,128)} %bitcast.449), calls=%async_computation.9 | async-start | bytes 4194304 | tf_op jit(solution)/shard_map/all_to_all | solution.py:114
  224.7 2.2 fusion.50
  226.9 2.3 fusion.52
  235.4 2.6 convolution_add_fusion.3
  237.9 15.1 %all-to-all-done.9 = f32[32,128,128]{2,1,0:T(8,128)} async-done(((f32[32,128,128]{2,1,0:T(8,128)}), f32[32,128,128]{2,1,0:T(8,128)}, u32[]{:S(2)}, u32[]{:S(2)}) %all-to-all-start.9) | async-done | bytes 2097184 | tf_op jit(solution)/shard_map/all_to_all | solution.py:114
  253.0 4.5 %all-to-all-start.8 = ((f32[32,128,128]{2,1,0:T(8,128)}), f32[32,128,128]{2,1,0:T(8,128)S(1)}, u32[]{:S(2)}, u32[]{:S(2)}) async-start(f32[32,128,128]{2,1,0:T(8,128)} %bitcast.433), calls=%async_computation.8 | async-start | bytes 4194304 | tf_op jit(solution)/shard_map/all_to_all | solution.py:113
  258.9 1.8 bitcast_reduce_fusion
  261.7 24.2 %all-to-all-done.8 = f32[32,128,128]{2,1,0:T(8,128)S(1)} async-done(((f32[32,128,128]{2,1,0:T(8,128)}), f32[32,128,128]{2,1,0:T(8,128)S(1)}, u32[]{:S(2)}, u32[]{:S(2)}) %all-to-all-start.8) | async-done | bytes 2097184 | tf_op jit(solution)/shard_map/all_to_all | solution.py:113
  (246 shorter events, 80.2 us)
Async XLA Ops:
  0.6 21.9 %copy-start = (bf16[128,1024]{1,0:T(8,128)(2,1)S(1)}, bf16[128,1024]{1,0:T(8,128)(2,1)}, u32[]{:S(2)}) copy-start(bf16[128,1024]{1,0:T(8,128)(2,1)} %param.46) | copy-start | bytes 786436
  0.6 34.5 %copy-start.48 = (bf16[128,1024]{1,0:T(8,128)(2,1)S(1)}, bf16[128,1024]{1,0:T(8,128)(2,1)}, u32[]{:S(2)}) copy-start(bf16[128,1024]{1,0:T(8,128)(2,1)} %param.44) | copy-start | bytes 786436
  2.1 16.3 %all-to-all-start.4 = ((bf16[1,32,1]{2,0,1:T(2,128)(2,1)}), bf16[1,32,1]{2,0,1:T(2,128)(2,1)S(1)}, u32[]{:S(2)}, u32[]{:S(2)}) async-start(bf16[1,32,1]{2,0,1:T(2,128)(2,1)} %broadcast_in_dim.125), calls=%async_computation.4 | async-start | bytes 32768 | tf_op jit(solution)/shard_map/all_to_all | solution.py:54
  18.4 11.1 %all-to-all-start.1 = ((bf16[1,32,1]{2,0,1:T(2,128)(2,1)}), bf16[1,32,1]{2,0,1:T(2,128)(2,1)S(1)}, u32[]{:S(2)}, u32[]{:S(2)}) async-start(bf16[1,32,1]{2,0,1:T(2,128)(2,1)} %broadcast_in_dim.124), calls=%async_computation.1 | async-start | bytes 32768 | tf_op jit(solution)/shard_map/all_to_all | solution.py:51
  30.8 26.6 %copy-start.28 = (bf16[128,4096]{1,0:T(8,128)(2,1)S(1)}, bf16[128,4096]{1,0:T(8,128)(2,1)}, u32[]{:S(2)}) copy-start(bf16[128,4096]{1,0:T(8,128)(2,1)} %param.43) | copy-start | bytes 3145732
  30.8 21.4 %all-to-all-start.3 = ((bf16[128,32,128]{2,0,1:T(8,128)(2,1)}), bf16[128,32,128]{2,0,1:T(8,128)(2,1)S(1)}, u32[]{:S(2)}, u32[]{:S(2)}) async-start(bf16[128,32,128]{2,0,1:T(8,128)(2,1)} %bitcast.9), calls=%async_computation.3 | async-start | bytes 2097152 | tf_op jit(solution)/shard_map/all_to_all | solution.py:48
  52.2 75.0 %copy-start.11 = (bf16[128,32,128]{2,0,1:T(8,128)(2,1)}, bf16[128,32,128]{2,0,1:T(8,128)(2,1)S(1)}, u32[]{:S(2)}) copy-start(bf16[128,32,128]{2,0,1:T(8,128)(2,1)S(1)} %all-to-all-done.3) | copy-start | bytes 3145732
  53.5 20.9 %all-to-all-start = ((bf16[128,32,128]{2,0,1:T(8,128)(2,1)}), bf16[128,32,128]{2,0,1:T(8,128)(2,1)S(1)}, u32[]{:S(2)}, u32[]{:S(2)}) async-start(bf16[128,32,128]{2,0,1:T(8,128)(2,1)} %bitcast), calls=%async_computation | async-start | bytes 2097152 | tf_op jit(solution)/shard_map/all_to_all | solution.py:45
  74.3 47.4 %copy-start.13 = (bf16[128,32,128]{2,0,1:T(8,128)(2,1)}, bf16[128,32,128]{2,0,1:T(8,128)(2,1)S(1)}, u32[]{:S(2)}) copy-start(bf16[128,32,128]{2,0,1:T(8,128)(2,1)S(1)} %all-to-all-done) | copy-start | bytes 3145732
  74.3 20.9 %all-to-all-start.2 = ((bf16[128,32,128]{0,2,1:T(8,128)(2,1)}), bf16[128,32,128]{0,2,1:T(8,128)(2,1)S(1)}, u32[]{:S(2)}, u32[]{:S(2)}) async-start(bf16[128,32,128]{0,2,1:T(8,128)(2,1)} %bitcast.439), calls=%async_computation.2 | async-start | bytes 2097152 | tf_op jit(solution)/shard_map/all_to_all | solution.py:61
  96.2 20.9 %all-to-all-start.5 = ((bf16[128,32,128]{0,2,1:T(8,128)(2,1)}), bf16[128,32,128]{0,2,1:T(8,128)(2,1)S(1)}, u32[]{:S(2)}, u32[]{:S(2)}) async-start(bf16[128,32,128]{0,2,1:T(8,128)(2,1)} %bitcast.438), calls=%async_computation.5 | async-start | bytes 2097152 | tf_op jit(solution)/shard_map/all_to_all | solution.py:62
  117.1 7.2 %copy-start.15 = (bf16[128,32,128]{0,2,1:T(8,128)(2,1)}, bf16[128,32,128]{0,2,1:T(8,128)(2,1)S(1)}, u32[]{:S(2)}) copy-start(bf16[128,32,128]{0,2,1:T(8,128)(2,1)S(1)} %all-to-all-done.5) | copy-start | bytes 3145732
  117.1 21.4 %all-to-all-start.6 = ((bf16[128,32,128]{0,2,1:T(8,128)(2,1)}), bf16[128,32,128]{0,2,1:T(8,128)(2,1)}, u32[]{:S(2)}, u32[]{:S(2)}) async-start(bf16[128,32,128]{0,2,1:T(8,128)(2,1)} %bitcast.436), calls=%async_computation.6 | async-start | bytes 2097152 | tf_op jit(solution)/shard_map/all_to_all | solution.py:63
  129.1 11.8 %copy-start.42 = (bf16[4,128,128]{2,1,0:T(8,128)(2,1)S(1)}, bf16[4,128,128]{2,1,0:T(8,128)(2,1)}, u32[]{:S(2)}) copy-start(bf16[4,128,128]{2,1,0:T(8,128)(2,1)} %slice.532) | copy-start | bytes 393220
  142.4 3.1 %copy-start.40 = (bf16[4,128,128]{1,2,0:T(8,128)(2,1)S(1)}, bf16[4,128,128]{1,2,0:T(8,128)(2,1)}, u32[]{:S(2)}) copy-start(bf16[4,128,128]{1,2,0:T(8,128)(2,1)} %get-tuple-element.221) | copy-start | bytes 393220
  144.4 44.0 %copy-start.30 = (bf16[4,128,128]{2,1,0:T(8,128)(2,1)}, bf16[4,128,128]{2,1,0:T(8,128)(2,1)S(1)}, u32[]{:S(2)}) copy-start(bf16[4,128,128]{2,1,0:T(8,128)(2,1)S(1)} %copy.82) | copy-start | bytes 393220
  144.6 34.5 %copy-start.32 = (bf16[4,128,128]{2,1,0:T(8,128)(2,1)}, bf16[4,128,128]{2,1,0:T(8,128)(2,1)S(1)}, u32[]{:S(2)}) copy-start(bf16[4,128,128]{2,1,0:T(8,128)(2,1)S(1)} %copy.80) | copy-start | bytes 393220
  145.5 21.1 %copy-start.34 = (bf16[4,128,128]{2,1,0:T(8,128)(2,1)}, bf16[4,128,128]{2,1,0:T(8,128)(2,1)S(1)}, u32[]{:S(2)}) copy-start(bf16[4,128,128]{2,1,0:T(8,128)(2,1)S(1)} %copy.76) | copy-start | bytes 393220
  145.7 16.2 %copy-start.36 = (bf16[4,128,128]{2,1,0:T(8,128)(2,1)}, bf16[4,128,128]{2,1,0:T(8,128)(2,1)S(1)}, u32[]{:S(2)}) copy-start(bf16[4,128,128]{2,1,0:T(8,128)(2,1)S(1)} %copy.74) | copy-start | bytes 393220
  147.9 5.9 %copy-start.29 = (bf16[8,128,128]{2,1,0:T(8,128)(2,1)S(1)}, bf16[8,128,128]{2,1,0:T(8,128)(2,1)}, u32[]{:S(2)}) copy-start(bf16[8,128,128]{2,1,0:T(8,128)(2,1)} %slice.537) | copy-start | bytes 786436
  152.6 2.9 %copy-start.47 = (f32[512,128]{1,0:T(8,128)S(1)}, f32[512,128]{1,0:T(8,128)}, u32[]{:S(2)}) copy-start(f32[512,128]{1,0:T(8,128)} %fusion.100) | copy-start | bytes 786436
  178.4 3.1 %copy-start.6 = (bf16[512,3072]{0,1:T(8,128)(2,1)}, bf16[512,3072]{0,1:T(8,128)(2,1)S(1)}, u32[]{:S(2)}) copy-start(bf16[512,3072]{0,1:T(8,128)(2,1)S(1)} %fusion.25) | copy-start | bytes 9437188
  189.8 3.3 %copy-start.17 = (f32[1,512,4096]{1,2,0:T(8,128)}, f32[1,512,4096]{1,2,0:T(8,128)S(1)}, u32[]{:S(2)}) copy-start(f32[1,512,4096]{1,2,0:T(8,128)S(1)} %get-tuple-element.256) | copy-start | bytes 25165828
  189.8 3.3 %copy-start.49 = (bf16[4,128,128]{2,1,0:T(8,128)(2,1)S(1)}, bf16[4,128,128]{2,1,0:T(8,128)(2,1)}, u32[]{:S(2)}) copy-start(bf16[4,128,128]{2,1,0:T(8,128)(2,1)} %copy.83) | copy-start | bytes 393220
  198.9 21.0 %all-to-all-start.7 = ((bf16[32,128,128]{1,2,0:T(8,128)(2,1)}), bf16[32,128,128]{1,2,0:T(8,128)(2,1)S(1)}, u32[]{:S(2)}, u32[]{:S(2)}) async-start(bf16[32,128,128]{1,2,0:T(8,128)(2,1)} %copy.84), calls=%async_computation.7 | async-start | bytes 2097152 | tf_op jit(solution)/shard_map/all_to_all | solution.py:111
  210.0 14.6 %copy-start.39 = (bf16[4,128,128]{2,1,0:T(8,128)(2,1)S(1)}, bf16[4,128,128]{2,1,0:T(8,128)(2,1)}, u32[]{:S(2)}) copy-start(bf16[4,128,128]{2,1,0:T(8,128)(2,1)} %copy.72) | copy-start | bytes 393220
  220.0 6.9 %copy-start.37 = (bf16[4,128,128]{2,1,0:T(8,128)(2,1)S(1)}, bf16[4,128,128]{2,1,0:T(8,128)(2,1)}, u32[]{:S(2)}) copy-start(bf16[4,128,128]{2,1,0:T(8,128)(2,1)} %copy-done.36) | copy-start | bytes 393220
  220.0 33.1 %all-to-all-start.9 = ((f32[32,128,128]{2,1,0:T(8,128)}), f32[32,128,128]{2,1,0:T(8,128)}, u32[]{:S(2)}, u32[]{:S(2)}) async-start(f32[32,128,128]{2,1,0:T(8,128)} %bitcast.449), calls=%async_computation.9 | async-start | bytes 4194304 | tf_op jit(solution)/shard_map/all_to_all | solution.py:114
  224.7 4.5 %copy-start.10 = (bf16[512,2560]{0,1:T(8,128)(2,1)S(1)}, bf16[512,2560]{0,1:T(8,128)(2,1)}, u32[]{:S(2)}) copy-start(bf16[512,2560]{0,1:T(8,128)(2,1)} %copy-done.9) | copy-start | bytes 7864324
  224.7 4.5 %copy-start.35 = (bf16[4,128,128]{2,1,0:T(8,128)(2,1)S(1)}, bf16[4,128,128]{2,1,0:T(8,128)(2,1)}, u32[]{:S(2)}) copy-start(bf16[4,128,128]{2,1,0:T(8,128)(2,1)} %copy-done.34) | copy-start | bytes 393220
  253.0 32.9 %all-to-all-start.8 = ((f32[32,128,128]{2,1,0:T(8,128)}), f32[32,128,128]{2,1,0:T(8,128)S(1)}, u32[]{:S(2)}, u32[]{:S(2)}) async-start(f32[32,128,128]{2,1,0:T(8,128)} %bitcast.433), calls=%async_computation.8 | async-start | bytes 4194304 | tf_op jit(solution)/shard_map/all_to_all | solution.py:113
  257.6 29.5 %copy-start.1 = (bf16[128,1024]{1,0:T(8,128)(2,1)S(1)}, bf16[128,1024]{1,0:T(8,128)(2,1)}, u32[]{:S(2)}) copy-start(bf16[128,1024]{1,0:T(8,128)(2,1)} %param.46) | copy-start | bytes 786436
  (52 other events, 80.8 us)
where the time goes:
time: 293 us; the launch traced here: 287 us
  waiting for transfers between devices  127 us (43%)
  matrix products  48.4 us (17%)
  starting transfers between devices  47.8 us (16%)
  local copies, waits for them, and re-layouts  47.2 us (16%)
  other arithmetic  14.9 us (5%)
    all_to_all x1, waiting for transfers between devices, per_device(): lax.all_to_all(key_acc, 'seq', split_axis=0, concat_axis=1, tiled=True)  24.2 us
    unnamed x141, local copies, waits for them, and re-layouts  22.6 us
    all_to_all x1, waiting for transfers between devices, per_device(): lax.all_to_all(spread_kv(value_code_matrix, HEAD_WIDTH), 'seq', split_axi...  16.9 us
    all_to_all x1, waiting for transfers between devices, per_device(): lax.all_to_all(spread_kv(key_codes, HEAD_WIDTH), 'seq', split_axis=1, con...  15.6 us
    all_to_all x1, waiting for transfers between devices, per_device(): lax.all_to_all(value_acc, 'seq', split_axis=0, concat_axis=1, tiled=True)  15.1 us
    all_to_all x1, waiting for transfers between devices, per_device(): lax.all_to_all(queries, 'seq', split_axis=1, concat_axis=0, tiled=True)  14.6 us
    dot_general x8, matrix products, per_device(): jnp.einsum('hqk,qhd->kd', prob_bf, grad_blk, preferred_element_type=jnp.f...  13.5 us
    dot_general x8, matrix products, per_device(): jnp.einsum('qhd,kd->hqk', grad_blk, value_blk, preferred_element_type=jnp...  11.8 us
  transfers between devices with their start and end apart: 10, of which 10 were waited for; matrix products, arithmetic and copies ran while one was open for 14% of the time, Pallas kernels for 0%

commit v1 on v0

v1 whole, which is shorter than its diff:
```python
import jax
import jax.numpy as jnp
from jax import lax
from jax.experimental import pallas as pl
from jax.experimental.pallas import tpu as pltpu
from jax.sharding import PartitionSpec as P

F32, BF = jnp.float32, jnp.bfloat16
W = 128
SC = W ** -0.5
C2 = SC * 1.4426950408889634
CH = 512
MESH = pl.DeviceIdType.MESH


def dot(a, b):
    return jnp.dot(a, b, preferred_element_type=F32)


def kernel(
    q_in, k_in, ks_in, v_in, vs_in, o_in, g_in,
    dq_out, dk_out, dv_out,
    gl, ol, kl, vl, ksl, vsl, dts, kvs,
    kv, kt, qbuf, gbuf, de,
    sbuf, qt, gt, qn, gn, dqt, ml,
    acc, dqs, rbuf1, fs, rbuf2, fb,
    lsem, s1s, kvr, f1s, f2s, f3s, qs, qr, gs, gr, des, der, dqss, dqr,
    r1s, r1r, r2s, r2r, dks, dvs, dkr, dvr,
):
    dp = lax.axis_index("dp")
    s = lax.axis_index("seq")
    x, z, core = s // 8, (s // 2) % 4, s % 2
    b = ((z + 1) // 2) % 2
    me = x * 4 + (z // 2) * 2 + core
    grp = me // 2
    other = s + 1 - 2 * core
    partner = x * 8 + (2 * (z // 2) + 1 - z % 2) * 2 + core

    def seq_in(n, bb):
        return (n // 4) * 8 + (bb + ((n // 2) % 2) * (3 - 2 * bb)) * 2 + n % 2

    def seq_of(n):
        return seq_in(n, b)

    def rcopy(src, dst, ssem, rsem, dev):
        return pltpu.make_async_remote_copy(
            src_ref=src, dst_ref=dst, send_sem=ssem, recv_sem=rsem,
            device_id=(dp, dev), device_id_type=MESH,
        )

    def arrived(dst, sem):
        pltpu.make_async_copy(dst, dst, sem).wait()

    def loop(n, f, start=0):
        def body(i, c):
            f(i)
            return c
        lax.fori_loop(start, n, body, 0)

    def cols(n, w):
        return pl.ds(pl.multiple_of(n * w, w), w)

    local = [
        pltpu.make_async_copy(a, c, lsem.at[i])
        for i, (a, c) in enumerate(
            ((k_in, kl), (ks_in, ksl), (v_in, vl), (vs_in, vsl), (g_in, gl), (o_in, ol))
        )
    ]
    for c in local:
        c.start()
    barrier = pltpu.get_barrier_semaphore()

    def greet(k):
        pl.semaphore_signal(
            barrier, inc=1, device_id=(dp, seq_of((me + k) % 16)), device_id_type=MESH
        )
    loop(16, greet, 1)
    pl.semaphore_signal(barrier, inc=1, device_id=(dp, partner), device_id_type=MESH)

    for c in local[:4]:
        c.wait()
    for i, (codes, scales) in enumerate(((kl, ksl), (vl, vsl))):
        sc = scales[...].astype(F32)
        for g in range(8):
            kvs[g, i] = (codes[:, W * g:W * g + W].astype(F32) * sc[0:1, g:g + 1]).astype(BF)
    for c in local[4:]:
        c.wait()
    lane = lax.broadcasted_iota(jnp.int32, (W, W), 1)
    dmat = jnp.zeros((W, W), F32)
    for h in range(32):
        hs = slice(W * h, W * h + W)
        prod = gl[:, hs].astype(F32) * ol[:, hs].astype(F32)
        dmat = jnp.where(lane == h, jnp.sum(prod, axis=1, keepdims=True), dmat)
    dts[...] = dmat.T

    pl.semaphore_wait(barrier, 16)

    def send_kv(k):
        g = (grp + k) % 8
        rcopy(kvs.at[g], kv.at[s], s1s.at[k], kvr.at[s], seq_of(g * 2 + core)).start()
    loop(8, send_kv, 1)
    pltpu.make_async_copy(kvs.at[grp], kv.at[s], kvr.at[s]).start()

    def send_rows(k):
        n = (me + k) % 16
        dev = seq_of(n)
        rcopy(q_in.at[:, cols(n, 256)], qbuf.at[me], qs.at[k], qr.at[me], dev).start()
        rcopy(g_in.at[:, cols(n, 256)], gbuf.at[me], gs.at[k], gr.at[me], dev).start()
        rcopy(dts.at[cols(n // 4, 8)], de.at[me], des.at[k], der.at[me], dev).start()
    loop(16, send_rows, 1)
    pltpu.make_async_copy(q_in.at[:, cols(me, 256)], qbuf.at[me], qr.at[me]).start()
    pltpu.make_async_copy(g_in.at[:, cols(me, 256)], gbuf.at[me], gr.at[me]).start()
    pltpu.make_async_copy(dts.at[cols(me // 4, 8)], de.at[me], der.at[me]).start()

    def forward(k):
        j = seq_of(((grp + k) % 8) * 2 + core)
        arrived(kv.at[j], kvr.at[j])
        rcopy(kv.at[j], kv.at[j], f1s.at[k], kvr.at[j], partner).start()
        rcopy(kv.at[j], kv.at[j], f2s.at[k], kvr.at[j], other).start()
    loop(8, forward)

    def row(t):
        return seq_of(15 - t)

    def prep(u):
        w = u % 2
        for p in range(2):
            n = 15 - 2 * u - p
            arrived(qbuf.at[n], qr.at[n])
            arrived(gbuf.at[n], gr.at[n])
            arrived(de.at[n], der.at[n])
            for h in range(2):
                i = 2 * p + h
                q = qbuf[n, :, W * h:W * h + W]
                g = gbuf[n, :, W * h:W * h + W]
                qn[w, W * i:W * i + W, :] = q
                gn[w, W * i:W * i + W, :] = g
                qt[w, :, W * i:W * i + W] = q.T
                gt[w, :, W * i:W * i + W] = g.T
        ml[w, 0] = jnp.full((8, 512), -1e30, F32)
        ml[w, 1] = jnp.zeros((8, 512), F32)

    def chunk_of(i, c):
        return kv[pl.ds(4 * c, 4), i].reshape(CH, W)

    def stat(sv, w):
        m = ml[w, 0]
        s3 = sv.reshape(CH // 8, 8, 512)
        mn = jnp.maximum(m, jnp.max(s3, axis=0))
        ml[w, 1] = ml[w, 1] * jnp.exp2(m - mn) + jnp.sum(jnp.exp2(s3 - mn[None]), axis=0)
        ml[w, 0] = mn

    def part_a(c, u):
        w = u % 2
        sv = dot(chunk_of(0, c), qt[w]) * C2
        sbuf[w, cols(c, CH), :] = sv
        stat(sv, w)

    def last_a(u):
        w = u % 2
        c = 7 - u
        sv = dot(chunk_of(0, c), qt[w]) * C2
        kp = c * CH + lax.broadcasted_iota(jnp.int32, (CH, 512), 0)
        li = lax.broadcasted_iota(jnp.int32, (1, 512), 1)
        qp = jnp.where(li < 256, row(2 * u), row(2 * u + 1)) * W + (li & (W - 1))
        sv = jnp.where(kp <= qp, sv, -jnp.inf)
        sbuf[w, cols(c, CH), :] = sv
        stat(sv, w)

    def part_b(c, u, lse, delta):
        w = u % 2
        p = jnp.exp2(sbuf[w, cols(c, CH), :] - lse)
        dpr = dot(chunk_of(1, c), gt[w])
        ds = (p * (dpr - delta) * SC).astype(BF)
        pair = pl.ds(2 * c, 2)
        acc[1, pair] += dot(p.astype(BF), gn[w]).reshape(2, 2, W, W)
        acc[0, pair] += dot(ds, qn[w]).reshape(2, 2, W, W)
        dqt[...] += dot(kt[:, cols(c, CH)], ds)

    def begin(u):
        w = u % 2
        m, l = ml[w, 0], ml[w, 1]
        mm = jnp.max(m, axis=0, keepdims=True)
        lse = mm + jnp.log2(jnp.sum(l * jnp.exp2(m - mm), axis=0, keepdims=True))
        r0 = 2 * (me % 4)
        delta = jnp.concatenate(
            [de[15 - 2 * u - p, pl.ds(r0 + h, 1), :] for p in range(2) for h in range(2)], axis=1
        )
        dqt[...] = jnp.zeros((W, 512), F32)
        return lse, delta

    def stage1(c):
        rcopy(acc.at[:, pl.ds(2 * c, 2), 1 - core], rbuf1.at[c], r1s.at[c], r1r.at[c], other).start()

    def stage2(c):
        near = (c + b) % 2
        far = 1 - near
        arrived(rbuf1.at[c], r1r.at[c])
        for i in range(2):
            fs[c, i] = acc[i, 2 * c + far, core] + rbuf1[c, i, far]
        rcopy(fs.at[c], rbuf2.at[c], r2s.at[c], r2r.at[c], partner).start()
        for i in range(2):
            acc[i, 2 * c + near, core] += rbuf1[c, i, near]

    def stage3(c):
        near = (c + b) % 2
        own = c * 2 + core
        dev = seq_of(own)
        arrived(rbuf2.at[c], r2r.at[c])
        for i in range(2):
            fb[c, i] = (acc[i, 2 * c + near, core] + rbuf2[c, i]).astype(BF)
        for i, (out, ssem, rsem) in enumerate(((dk_out, dks, dkr), (dv_out, dvs, dvr))):
            dst = out.at[:, cols(grp, W)]

            @pl.when(own != me)
            def _():
                rcopy(fb.at[c, i], dst, ssem.at[c], rsem.at[grp], dev).start()

            @pl.when(own == me)
            def _():
                pltpu.make_async_copy(fb.at[c, i], dst, rsem.at[grp]).start()

    def end(u):
        for p in range(2):
            n = 15 - 2 * u - p
            for h in range(2):
                i = 2 * p + h
                dqs[n, :, W * h:W * h + W] = dqt[:, W * i:W * i + W].T.astype(BF)
            dst = dq_out.at[:, cols(me, 256)]

            @pl.when(n != me)
            def _():
                rcopy(dqs.at[n], dst, dqss.at[n], dqr.at[me], seq_of(n)).start()

            @pl.when(n == me)
            def _():
                pltpu.make_async_copy(dqs.at[n], dst, dqr.at[me]).start()
        stage1(7 - u)

        @pl.when(u >= 1)
        def _():
            stage2(8 - u)

        @pl.when(u >= 2)
        def _():
            stage3(9 - u)

    def clear(j):
        for i in range(2):
            acc[i, j] = jnp.zeros((2, W, W), F32)
    loop(16, clear)
    prep(0)

    def first(xx):
        for zz in range(2):
            j = seq_in(xx * 4 + zz * 2 + core, 1 - b)
            arrived(kv.at[j], kvr.at[j])
            rcopy(kv.at[j], kv.at[j], f3s.at[2 * xx + zz], kvr.at[j], other).start()
        for zz in range(4):
            j = xx * 8 + zz * 2 + 1 - core
            arrived(kv.at[j], kvr.at[j])
        for i in range(2):
            c = 2 * xx + i
            kt[:, cols(c, CH)] = chunk_of(0, c).T

        part_a(2 * xx, 0)

        @pl.when(xx < 3)
        def _():
            part_a(2 * xx + 1, 0)
    loop(4, first)
    last_a(0)

    def step(u):
        lse, delta = begin(u)
        prep(u + 1)

        def main(c):
            part_b(c, u, lse, delta)
            part_a(c, u + 1)
        loop(6 - u, main)
        part_b(6 - u, u, lse, delta)
        last_a(u + 1)
        part_b(7 - u, u, lse, delta)
        end(u)
    loop(7, step)
    lse, delta = begin(7)
    part_b(0, 7, lse, delta)
    end(7)
    stage2(0)
    stage3(1)
    stage3(0)

    def finish(n):
        arrived(dq_out.at[:, cols(n, 256)], dqr.at[n])

        @pl.when(n != me)
        def _():
            rcopy(dqs.at[n], dqs.at[n], dqss.at[n], dqr.at[n], other).wait_send()
    loop(16, finish)

    def finish8(c):
        arrived(dk_out.at[:, cols(c, W)], dkr.at[c])
        arrived(dv_out.at[:, cols(c, W)], dvr.at[c])
        rcopy(fs.at[c], fs.at[c], r2s.at[c], r2r.at[c], other).wait_send()
        rcopy(rbuf1.at[c], rbuf1.at[c], r1s.at[c], r1r.at[c], other).wait_send()
        rcopy(kv.at[0], kv.at[0], f1s.at[c], kvr.at[0], other).wait_send()
        rcopy(kv.at[0], kv.at[0], f2s.at[c], kvr.at[0], other).wait_send()
        rcopy(kv.at[0], kv.at[0], f3s.at[c], kvr.at[0], other).wait_send()

        @pl.when(c * 2 + core != me)
        def _():
            rcopy(fb.at[c, 0], fb.at[c, 0], dks.at[c], dkr.at[c], other).wait_send()
            rcopy(fb.at[c, 1], fb.at[c, 1], dvs.at[c], dvr.at[c], other).wait_send()

        @pl.when(c >= 1)
        def _():
            rcopy(kvs.at[0], kvs.at[0], s1s.at[c], kvr.at[0], other).wait_send()
    loop(8, finish8)

    def finish15(k):
        rcopy(qbuf.at[0], qbuf.at[0], qs.at[k], qr.at[0], other).wait_send()
        rcopy(gbuf.at[0], gbuf.at[0], gs.at[k], gr.at[0], other).wait_send()
        rcopy(de.at[0], de.at[0], des.at[k], der.at[0], other).wait_send()
    loop(16, finish15, 1)


def per_device(q, kc, ks, vc, vs, o, g):
    any_ = pl.BlockSpec(memory_space=pl.ANY)
    vm, dma = pltpu.VMEM, pltpu.SemaphoreType.DMA
    rows, qc = q.shape
    kc_cols = kc.shape[1]
    return pl.pallas_call(
        kernel,
        out_shape=[
            jax.ShapeDtypeStruct(q.shape, BF),
            jax.ShapeDtypeStruct(kc.shape, BF),
            jax.ShapeDtypeStruct(vc.shape, BF),
        ],
        in_specs=[any_] * 7,
        out_specs=[any_] * 3,
        scratch_shapes=[
            vm((rows, qc), BF), vm((rows, qc), BF), vm((rows, kc_cols), BF), vm((rows, kc_cols), BF),
            vm((1, 8), BF), vm((1, 8), BF), vm((W, W), F32), vm((8, 2, W, W), BF),
            vm((32, 2, W, W), BF), vm((W, 32 * W), BF),
            vm((16, W, 256), BF), vm((16, W, 256), BF), vm((16, 8, W), F32),
            vm((2, 32 * W, 512), F32),
            vm((2, W, 512), BF), vm((2, W, 512), BF), vm((2, 512, W), BF), vm((2, 512, W), BF),
            vm((W, 512), F32), vm((2, 2, 8, 512), F32),
            vm((2, 16, 2, W, W), F32), vm((16, W, 256), BF),
            vm((8, 2, 2, W, W), F32), vm((8, 2, W, W), F32), vm((8, 2, W, W), F32),
            vm((8, 2, W, W), BF),
            dma((6,)), dma((8,)), dma((32,)), dma((8,)), dma((8,)), dma((8,)),
            dma((16,)), dma((16,)), dma((16,)), dma((16,)), dma((16,)), dma((16,)),
            dma((16,)), dma((16,)),
            dma((8,)), dma((8,)), dma((8,)), dma((8,)), dma((8,)), dma((8,)), dma((8,)), dma((8,)),
        ],
        compiler_params=pltpu.CompilerParams(
            collective_id=0, has_side_effects=True, vmem_limit_bytes=56 * 2**20
        ),
        cost_estimate=pl.CostEstimate(
            flops=11_000_000_000, bytes_accessed=8_000_000, transcendentals=18_000_000
        ),
    )(q, kc, ks, vc, vs, o, g)


def solution(mesh):
    spec = P(("dp", "seq"), None)
    return jax.shard_map(
        per_device, mesh=mesh, in_specs=(spec,) * 7, out_specs=(spec,) * 3, check_vma=False
    )
```

time: 293 us -> 113 us (0.39); the launches traced: 287 us -> 113 us
  waiting for transfers between devices: 127 us -> 0 us
  Pallas kernels: 0 us -> 108 us
  matrix products: 48.4 us -> 0 us
  starting transfers between devices: 47.8 us -> 0 us
  local copies, waits for them, and re-layouts: 47.2 us -> 4.08 us
  other arithmetic: 14.9 us -> 0 us
    all_to_all x10 -> x0, waiting for transfers between devices: 127 us -> none  [the longest x1 24.2 us: per_device(): lax.all_to_all(key_acc, 'seq', split_axis=0, concat_axis=1, tiled=True)]
    pallas_call x0 -> x1, Pallas kernels: none -> 108 us  [per_device(): pl.pallas_call(kernel, out_shape=[jax.ShapeDtypeStruct(q.shape, BF), jax....]
    dot_general x40 -> x0, matrix products: 48.4 us -> none  [the longest x8 13.5 us: per_device(): jnp.einsum('hqk,qhd->kd', prob_bf, grad_blk, preferred_element_type=jnp.f...]
    all_to_all x10 -> x0, starting transfers between devices: 47.8 us -> none  [the longest x1 9.43 us: per_device(): lax.all_to_all(spread_kv(value_block_scale, 1), 'seq', split_axis=1, conc...]
    unnamed x141 -> x7, local copies, waits for them, and re-layouts: 22.6 us -> 4.08 us
    slice x39 -> x0, local copies, waits for them, and re-layouts: 15.5 us -> none  [the longest x9 5.57 us: per_device(): grad_blk = grad_heads[first_row:last_row]]
    reduce_sum x11 -> x0, other arithmetic: 9.09 us -> none  [the longest x8 5.58 us: per_device(): row_total = jnp.sum(expo, axis=2, keepdims=True)]
    broadcast_in_dim x8 -> x0, local copies, waits for them, and re-layouts: 5.5 us -> none  [spread_kv(): jnp.broadcast_to(split_pieces[:, :, None, :], (row_count_total, KEY_VALUE...]
  transfers between devices with their start and end apart: 10 -> 0, of which waited for: 10 -> 0; matrix products, arithmetic and copies ran while one was open for 14% -> 0% of each run, Pallas kernels for 0% -> 0%
where the time goes in v1:
time: 113 us
  Pallas kernels  108 us (96%)
  local copies, waits for them, and re-layouts  4.08 us (4%)
    pallas_call x1, Pallas kernels, per_device(): pl.pallas_call(kernel, out_shape=[jax.ShapeDtypeStruct(q.shape, BF), jax....  108 us
    unnamed x7, local copies, waits for them, and re-layouts  4.08 us

profile of v1, /device:TPU:1, one launch (start us, length us, event | category | flops | bytes accessed | tf_op | source)
XLA Modules:
  0.0 112.7 jit_solution(1258154789297229363)
XLA Ops:
  0.6 108.0 %shard_map.94 = (bf16[128,4096]{1,0:T(8,128)(2,1)}, bf16[128,1024]{1,0:T(8,128)(2,1)}, bf16[128,1024]{1,0:T(8,128)(2,1)}) custom-call(bf16[128,4096]{1,0:T(8,128)(2,1)} %q_in.1, bf16[128,1024]{1,0:T(8,128)(2,1)} %k_in.1, bf16[1,8]{1,0:T(2,128)(2,1)} %ks_in.1, bf16[128,1024]{1,0:T(8,128)(2,1)} %v_in.1, bf16[1,8]{1,0:T(2,128)(2,1)} %vs_in.1, ...), custom_call_target="tpu_custom_call" | custom-call | flops 11000000512 | bytes 8000000 | tf_op jit(solution)/shard_map/pallas_call | solution.py:333
  108.6 0.0 copy-start.1
  108.6 2.3 %copy.13 = bf16[128,4096]{1,0:T(8,128)(2,1)} copy(bf16[128,4096]{1,0:T(8,128)(2,1)} %get-tuple-element.6) | data formatting | bytes 2097152
  111.0 0.0 copy-done.1
  111.0 0.0 copy-start
  111.0 0.7 copy.14
  111.7 0.3 copy-done
  112.0 0.7 copy.15
Async XLA Ops:
  108.6 2.3 %copy-start.1 = (bf16[128,1024]{1,0:T(8,128)(2,1)S(1)}, bf16[128,1024]{1,0:T(8,128)(2,1)}, u32[]{:S(2)}) copy-start(bf16[128,1024]{1,0:T(8,128)(2,1)} %get-tuple-element.7) | copy-start | bytes 786436
  111.0 1.0 copy-start
